TPU v7x, 256 devices: a whole 4x4x8 slice. The times are simulated.
256 devices in a mesh: seq: 32 (over x, z), head: 8 (over y, core).
Axes of the slice: x: 4, y: 4, z: 8, core: 2. Of those that a mesh axis runs over, the one named last changes fastest.
Arguments:
- queries: bfloat16 [8192, 6144], P('seq', 'head'), may hold values from -32 to 32
- keys: bfloat16 [32768, 6144], P('seq', 'head'), may hold values from -32 to 32
- values: bfloat16 [32768, 6144], P('seq', 'head'), may hold values from -6 to 6
- query_cluster: int32 [8192], P('seq'), may hold values from 0 to 127, as said below
- key_cluster: int32 [32768], P('seq'), may hold values from 0 to 127, as said below
- cluster_owner: int32 [128], replicated, may hold values from 0 to 31, as said below
- pair_list: int32 [48, 128, 2], P('head'), may hold values from 0 to 127, as said below
- out_weight: bfloat16 [6144, 6144], P('head', 'seq'), may hold values from -0.15625 to 0.15625
Outputs:
- mixed: bfloat16 [8192, 6144], P('seq', 'head')
Inputs may be any that keep to these rules, and one draw needn't show every extreme that they name: cluster_owner[query_cluster[i]] takes each seq index at most 16 times within each aligned block of 256 tokens; one owner takes exactly 16 in every block. cluster_owner[key_cluster[j]] takes each seq index at most 64 times within each aligned block of 1024 tokens; one owner takes exactly 64 in every block. `cluster_owner`: each seq index owns exactly 4 clusters. pair_list[h, a] names 2 distinct clusters, all owned by the owner of cluster a.
All inputs are finite; a program needn't handle non-finite values.
Results may differ from a plain program's by a relative error of at most 0.0057.
Values may be sent and summed in bfloat16 or wider, within the bound.
A program may use at most 128 MiB of HBM per device.

v0:
```python
import math

import jax
import jax.numpy as jnp
from jax import lax
from jax.sharding import PartitionSpec as P


def onehot_rows(labels, count, dtype):
    return (labels[:, None] == jnp.arange(count, dtype=jnp.int32)[None, :]).astype(dtype)


def route(cluster_ids, cluster_owner, destinations):
    clusters = cluster_owner.shape[0]
    matches = cluster_ids[:, None] == jnp.arange(clusters, dtype=jnp.int32)[None, :]
    owners = jnp.sum(jnp.where(matches, cluster_owner[None, :], 0), axis=1)
    indicator = onehot_rows(owners, destinations, jnp.int32)
    slot_rank = jnp.sum(jnp.cumsum(indicator, axis=0) * indicator, axis=1) - 1
    return (owners, slot_rank)


def pack_rows(rows, owners, slot_rank, destinations, capacity):
    holder = jnp.zeros((destinations, capacity) + rows.shape[1:], rows.dtype)
    return holder.at[owners, slot_rank].set(rows)


def pack_labels(labels, owners, slot_rank, destinations, capacity):
    holder = jnp.full((destinations, capacity), -1, jnp.int32)
    return holder.at[owners, slot_rank].set(labels)


def attend(query_slots, query_labels, key_slots, value_slots, key_labels, allowed):
    heads_here = allowed.shape[0]
    clusters = allowed.shape[1]
    sources, count, feature_width = query_slots.shape
    head_size = feature_width // heads_here
    query_heads = jnp.transpose(
        query_slots.reshape(sources * count, heads_here, head_size), (1, 0, 2)
    )
    key_heads = jnp.transpose(key_slots.reshape(-1, heads_here, head_size), (1, 0, 2))
    value_heads = jnp.transpose(value_slots.reshape(-1, heads_here, head_size), (1, 0, 2))
    query_hot = onehot_rows(query_labels.reshape(-1), clusters, jnp.bfloat16)
    key_hot = onehot_rows(key_labels.reshape(-1), clusters, jnp.bfloat16)
    score_scale = 1.0 / math.sqrt(head_size)

    def one_head(operands):
        query_part, key_part, value_part, pair_table = operands
        selected = jnp.dot(query_hot, pair_table, preferred_element_type=jnp.float32).astype(
            jnp.bfloat16
        )
        visible = jnp.dot(selected, key_hot.T, preferred_element_type=jnp.float32) > 0.5
        scores = jnp.dot(query_part, key_part.T, preferred_element_type=jnp.float32) * score_scale
        largest = jnp.maximum(jnp.max(jnp.where(visible, scores, -jnp.inf), axis=1), 0.0)
        weights = jnp.where(visible, jnp.exp(scores - largest[:, None]), 0.0)
        total = jnp.exp(-largest) + jnp.sum(weights, axis=1)
        probs = (weights / total[:, None]).astype(jnp.bfloat16)
        return jnp.dot(probs, value_part, preferred_element_type=jnp.float32).astype(jnp.bfloat16)

    outputs = lax.map(one_head, (query_heads, key_heads, value_heads, allowed))
    return jnp.transpose(outputs, (1, 0, 2)).reshape(sources, count, feature_width)


def per_device(
    queries, keys, values, query_cluster, key_cluster, cluster_owner, pair_list, out_weight
):
    destinations = lax.axis_size("seq")
    query_capacity = 2 * queries.shape[0] // destinations
    key_capacity = 2 * keys.shape[0] // destinations
    clusters = cluster_owner.shape[0]
    allowed = jnp.any(
        pair_list[:, :, :, None] == jnp.arange(clusters, dtype=jnp.int32)[None, None, None, :],
        axis=2,
    ).astype(jnp.bfloat16)
    query_owner, query_rank = route(query_cluster, cluster_owner, destinations)
    key_owner, key_rank = route(key_cluster, cluster_owner, destinations)
    query_slots = pack_rows(queries, query_owner, query_rank, destinations, query_capacity)
    query_labels = pack_labels(query_cluster, query_owner, query_rank, destinations, query_capacity)
    key_slots = pack_rows(keys, key_owner, key_rank, destinations, key_capacity)
    value_slots = pack_rows(values, key_owner, key_rank, destinations, key_capacity)
    key_labels = pack_labels(key_cluster, key_owner, key_rank, destinations, key_capacity)
    got_key, got_value, got_klabel = (
        lax.all_to_all(key_slots, "seq", split_axis=0, concat_axis=0, tiled=True),
        lax.all_to_all(value_slots, "seq", split_axis=0, concat_axis=0, tiled=True),
        lax.all_to_all(key_labels, "seq", split_axis=0, concat_axis=0, tiled=True),
    )
    answered = attend(
        lax.all_to_all(query_slots, "seq", split_axis=0, concat_axis=0, tiled=True),
        lax.all_to_all(query_labels, "seq", split_axis=0, concat_axis=0, tiled=True),
        got_key,
        got_value,
        got_klabel,
        allowed,
    )
    returned = lax.all_to_all(answered, "seq", split_axis=0, concat_axis=0, tiled=True)
    attended = returned[query_owner, query_rank]
    terms = jnp.dot(
        attended,
        lax.all_gather(out_weight, "seq", axis=1, tiled=True),
        preferred_element_type=jnp.float32,
    )
    return lax.psum_scatter(terms, "head", scatter_dimension=1, tiled=True).astype(jnp.bfloat16)


def solution(mesh):
    in_specs = (
        P("seq", "head"),
        P("seq", "head"),
        P("seq", "head"),
        P("seq"),
        P("seq"),
        P(),
        P("head", None, None),
        P("head", "seq"),
    )
    out_specs = P("seq", "head")
    return jax.shard_map(
        per_device, mesh=mesh, in_specs=in_specs, out_specs=out_specs, check_vma=False
    )
```

profile of v0, /device:TPU:1, one launch (start us, length us, event | category | flops | bytes accessed | tf_op | source)
XLA Modules:
  0.0 494.2 jit_solution(2023313913685136478)
XLA Ops:
  8.4 21.7 %scatter_fusion = s32[32,16]{0,1:T(8,128)S(1)} fusion(s32[32,16]{0,1:T(8,128)S(1)} %broadcast_in_dim.42, s32[256]{0:T(256)S(1)} %bitcast.78, s32[256]{0:T(256)} %param.13), kind=kCustom, calls=%fused_computation.1 | custom fusion | bytes 5120 | tf_op jit(solution)/shard_map/scatter | solution.py:29
  30.8 11.9 %all-to-all-start = ((s32[32,1,16]{2,1,0:T(1,128)}), s32[32,1,16]{2,1,0:T(1,128)S(1)}, u32[]{:S(2)}, u32[]{:S(2)}) async-start(s32[32,1,16]{2,1,0:T(1,128)} %copy.32), calls=%async_computation | async-start | bytes 32768 | tf_op jit(solution)/shard_map/all_to_all | solution.py:88
  43.8 9.0 %reduce-window.16 = s32[32,8,128]{2,1,0:T(8,128)S(1)} reduce-window(s32[32,8,128]{2,1,0:T(8,128)S(1)} %fusion.41, s32[]{:T(128)} %copy.54), window={size=1x1x128 pad=0_0x0_0x127_0}, to_apply=%region_6.7 | reduce-window | flops 4161536 | bytes 262148 | tf_op jit(solution)/shard_map/reduce-window.2
  54.8 4.5 scatter_custom_fusion.2
  60.0 9.2 %all-to-all-start.1 = ((s32[32,1,64]{2,1,0:T(1,128)}), s32[32,1,64]{2,1,0:T(1,128)S(1)}, u32[]{:S(2)}, u32[]{:S(2)}) async-start(s32[32,1,64]{2,1,0:T(1,128)} %all_to_all.26), calls=%async_computation.1 | async-start | bytes 32768 | tf_op jit(solution)/shard_map/all_to_all | solution.py:84
  70.2 34.2 %scatter_fusion.1 = bf16[32,16,768]{2,1,0:T(8,128)(2,1)} fusion(bf16[32,16,768]{2,1,0:T(8,128)(2,1)} %broadcast_in_dim.52, s32[256]{0:T(256)S(1)} %bitcast.79, bf16[256,768]{1,0:T(8,128)(2,1)S(1)} %copy-done.3), kind=kCustom, calls=%fused_computation.2 | custom fusion | bytes 1181696 | tf_op jit(solution)/shard_map/scatter | solution.py:24
  104.4 9.2 %all-to-all-start.2 = ((bf16[32,16,768]{2,1,0:T(8,128)(2,1)}), bf16[32,16,768]{2,1,0:T(8,128)(2,1)S(1)}, u32[]{:S(2)}, u32[]{:S(2)}) async-start(bf16[32,16,768]{2,1,0:T(8,128)(2,1)} %scatter_fusion.1), calls=%async_computation.2 | async-start | bytes 1572864 | tf_op jit(solution)/shard_map/all_to_all | solution.py:87
  113.6 7.9 %scatter_custom_fusion.3 = bf16[2048,768]{1,0:T(8,128)(2,1)} fusion(s32[1024]{0:T(1024)S(1)} %broadcast_select_fusion, bf16[1024,768]{1,0:T(8,128)(2,1)} %param.11, bf16[]{:T(256)} %constant.25.clone.1), kind=kCustom, calls=%fused_computation.42 | custom fusion | bytes 3146240
  121.5 10.8 %all-to-all-done.2 = bf16[32,16,768]{2,1,0:T(8,128)(2,1)S(1)} async-done(((bf16[32,16,768]{2,1,0:T(8,128)(2,1)}), bf16[32,16,768]{2,1,0:T(8,128)(2,1)S(1)}, u32[]{:S(2)}, u32[]{:S(2)}) %all-to-all-start.2) | async-done | bytes 786464 | tf_op jit(solution)/shard_map/all_to_all | solution.py:87
  133.2 8.5 %all-to-all-start.3 = ((bf16[32,64,768]{2,1,0:T(8,128)(2,1)}), bf16[32,64,768]{2,1,0:T(8,128)(2,1)S(1)}, u32[]{:S(2)}, u32[]{:S(2)}) async-start(bf16[32,64,768]{2,1,0:T(8,128)(2,1)} %bitcast.84), calls=%async_computation.3 | async-start | bytes 6291456 | tf_op jit(solution)/shard_map/all_to_all | solution.py:82
  141.7 7.9 %scatter_custom_fusion.4 = bf16[2048,768]{1,0:T(8,128)(2,1)} fusion(s32[1024]{0:T(1024)S(1)} %broadcast_select_fusion, bf16[1024,768]{1,0:T(8,128)(2,1)} %param.12, bf16[]{:T(256)} %constant.25.clone.1), kind=kCustom, calls=%fused_computation.40 | custom fusion | bytes 3146240
  149.7 62.8 %all-to-all-done.3 = bf16[32,64,768]{2,1,0:T(8,128)(2,1)S(1)} async-done(((bf16[32,64,768]{2,1,0:T(8,128)(2,1)}), bf16[32,64,768]{2,1,0:T(8,128)(2,1)S(1)}, u32[]{:S(2)}, u32[]{:S(2)}) %all-to-all-start.3) | async-done | bytes 3145760 | tf_op jit(solution)/shard_map/all_to_all | solution.py:82
  212.5 7.8 %all-to-all-start.4 = ((bf16[32,64,768]{2,1,0:T(8,128)(2,1)}), bf16[32,64,768]{2,1,0:T(8,128)(2,1)}, u32[]{:S(2)}, u32[]{:S(2)}) async-start(bf16[32,64,768]{2,1,0:T(8,128)(2,1)} %bitcast.83), calls=%async_computation.4 | async-start | bytes 6291456 | tf_op jit(solution)/shard_map/all_to_all | solution.py:83
  228.3 4.7 reshape.135
  233.0 4.2 copy.34
  237.3 64.7 %all-to-all-done.4 = bf16[32,64,768]{2,1,0:T(8,128)(2,1)} async-done(((bf16[32,64,768]{2,1,0:T(8,128)(2,1)}), bf16[32,64,768]{2,1,0:T(8,128)(2,1)}, u32[]{:S(2)}, u32[]{:S(2)}) %all-to-all-start.4) | async-done | bytes 3145760 | tf_op jit(solution)/shard_map/all_to_all | solution.py:83
  301.9 7.7 %reshape.136 = bf16[2048,6,128]{2,1,0:T(8,128)(2,1)} reshape(bf16[32,64,768]{2,1,0:T(8,128)(2,1)} %all-to-all-done.4) | data formatting | bytes 6291456 | tf_op jit(solution)/shard_map/reshape | solution.py:41
  309.7 4.3 copy.35
  314.0 82.4 %while.11 = (s32[]{:T(128)}, bf16[6,512,128]{2,1,0:T(8,128)(2,1)S(1)}, bf16[6,128,128]{2,1,0:T(8,128)(2,1)S(1)}, bf16[6,512,128]{2,1,0:T(8,128)(2,1)}, bf16[6,20...) while((s32[]{:T(128)}, ...), condition=%wide.region_17.18_spmd.clone, body=%wide.region_14.17_spmd.clone.sunk | while | flops 836502528 | bytes 38076540 | solution.py:59
  314.0 3.9 fusion.69
  317.9 3.7 select_reduce_fusion.4
  327.8 3.9 fusion.69
  331.7 3.7 select_reduce_fusion.4
  341.6 3.9 fusion.69
  355.3 3.9 fusion.69
  359.2 3.7 select_reduce_fusion.4
  369.1 3.9 fusion.69
  373.0 3.7 select_reduce_fusion.4
  382.8 3.9 fusion.69
  397.9 25.6 %all_to_all.38 = bf16[32,16,768]{2,1,0:T(8,128)(2,1)S(1)} all-to-all(bf16[32,16,768]{2,1,0:T(8,128)(2,1)S(1)} %reshape.137), channel_id=1, replica_groups=mesh['seq'=32,'head'=8] {'seq'}, dimensions={0} | all-to-all | bytes 1572864 | tf_op jit(solution)/shard_map/all_to_all | solution.py:94
  426.0 11.6 %fusion.53 = f32[256,6144]{1,0:T(8,128)} fusion(bf16[256,768]{1,0:T(8,128)(2,1)S(1)} %gather_fusion, bf16[768,6144]{0,1:T(8,128)(2,1)} %all-gather.2.cloned.1.call-done), kind=kOutput, calls=%fused_computation.83 | convolution fusion | flops 2415919104 | bytes 16121856 | tf_op jit(solution)/shard_map/dot_general | solution.py:96
  437.6 47.8 %reduce-scatter.2.cloned.1.call-done = f32[256,768]{1,0:T(8,128)} async-done(((f32[256,6144]{1,0:T(8,128)}), f32[256,768]{1,0:T(8,128)}) %reduce-scatter.2.cloned.1.call-update) | async-done | bytes 786448 | tf_op jit(solution)/shard_map/reduce_scatter | solution.py:101
  (94 shorter events, 65.9 us)
Async XLA Ops:
  6.5 63.6 %copy-start.3 = (bf16[256,768]{1,0:T(8,128)(2,1)S(1)}, bf16[256,768]{1,0:T(8,128)(2,1)}, u32[]{:S(2)}) copy-start(bf16[256,768]{1,0:T(8,128)(2,1)} %param.10) | copy-start | bytes 1179652
  30.8 29.2 %all-to-all-start = ((s32[32,1,16]{2,1,0:T(1,128)}), s32[32,1,16]{2,1,0:T(1,128)S(1)}, u32[]{:S(2)}, u32[]{:S(2)}) async-start(s32[32,1,16]{2,1,0:T(1,128)} %copy.32), calls=%async_computation | async-start | bytes 32768 | tf_op jit(solution)/shard_map/all_to_all | solution.py:88
  60.0 44.4 %all-to-all-start.1 = ((s32[32,1,64]{2,1,0:T(1,128)}), s32[32,1,64]{2,1,0:T(1,128)S(1)}, u32[]{:S(2)}, u32[]{:S(2)}) async-start(s32[32,1,64]{2,1,0:T(1,128)} %all_to_all.26), calls=%async_computation.1 | async-start | bytes 32768 | tf_op jit(solution)/shard_map/all_to_all | solution.py:84
  104.4 27.9 %all-to-all-start.2 = ((bf16[32,16,768]{2,1,0:T(8,128)(2,1)}), bf16[32,16,768]{2,1,0:T(8,128)(2,1)S(1)}, u32[]{:S(2)}, u32[]{:S(2)}) async-start(bf16[32,16,768]{2,1,0:T(8,128)(2,1)} %scatter_fusion.1), calls=%async_computation.2 | async-start | bytes 1572864 | tf_op jit(solution)/shard_map/all_to_all | solution.py:87
  132.3 0.9 copy-start.1
  133.2 79.3 %all-to-all-start.3 = ((bf16[32,64,768]{2,1,0:T(8,128)(2,1)}), bf16[32,64,768]{2,1,0:T(8,128)(2,1)S(1)}, u32[]{:S(2)}, u32[]{:S(2)}) async-start(bf16[32,64,768]{2,1,0:T(8,128)(2,1)} %bitcast.84), calls=%async_computation.3 | async-start | bytes 6291456 | tf_op jit(solution)/shard_map/all_to_all | solution.py:82
  141.7 79.3 %copy-start.4 = (s32[6,128,2]{1,2,0:T(2,128)S(1)}, s32[6,128,2]{1,2,0:T(2,128)}, u32[]{:S(2)}) copy-start(s32[6,128,2]{1,2,0:T(2,128)} %param.16) | copy-start | bytes 18436
  212.5 89.5 %all-to-all-start.4 = ((bf16[32,64,768]{2,1,0:T(8,128)(2,1)}), bf16[32,64,768]{2,1,0:T(8,128)(2,1)}, u32[]{:S(2)}, u32[]{:S(2)}) async-start(bf16[32,64,768]{2,1,0:T(8,128)(2,1)} %bitcast.83), calls=%async_computation.4 | async-start | bytes 6291456 | tf_op jit(solution)/shard_map/all_to_all | solution.py:83
  220.2 205.8 %all-gather.2.cloned.1.call-start = ((), (), s32[]{:S(2)}) async-start(), calls=%async_computation.7 | async-start | bytes 9732096 | tf_op jit(solution)/shard_map/all_gather | solution.py:98
  221.0 264.4 %reduce-scatter.2.cloned.1.call-start = ((), (), s32[]{:S(2)}) async-start(), calls=%async_computation.8 | async-start | bytes 7077888 | tf_op jit(solution)/shard_map/reduce_scatter | solution.py:101
  309.7 4.3 copy-start.2
  321.6 3.7 copy-start
  335.5 3.7 copy-start
  349.2 3.6 copy-start
  362.9 3.6 copy-start
  376.7 3.6 copy-start
  390.4 3.6 copy-start
Sparse Core Ops, SparseCore 0:
  223.6 125.5 all-gather.1
  437.8 47.5 reduce-scatter.1
where the time goes:
time: 497 us; the launch traced here: 494 us
  waiting for transfers between devices  187 us (38%)
  local copies, waits for them, and re-layouts  110 us (22%)
  matrix products  72 us (14%)
  starting transfers between devices  46.6 us (9%)
  other arithmetic  38.7 us (8%)
  blocking collectives  25.6 us (5%)
  between operations  13.7 us (3%)
    all_to_all x1, waiting for transfers between devices, per_device(): lax.all_to_all(value_slots, 'seq', split_axis=0, concat_axis=0, tiled=True)  64.7 us
    all_to_all x1, waiting for transfers between devices, per_device(): lax.all_to_all(key_slots, 'seq', split_axis=0, concat_axis=0, tiled=True)  62.8 us
    reduce_scatter x1, waiting for transfers between devices, per_device(): lax.psum_scatter(terms, 'head', scatter_dimension=1, tiled=True)  47.8 us
    scatter x1, local copies, waits for them, and re-layouts, pack_rows(): return holder.at[owners, slot_rank].set(rows)  34.2 us
    unnamed x14, local copies, waits for them, and re-layouts  32 us
    all_to_all x1, blocking collectives, per_device(): lax.all_to_all(answered, 'seq', split_axis=0, concat_axis=0, tiled=True)  25.6 us
    dot_general x6, matrix products, one_head(): jnp.dot(query_part, key_part.T, preferred_element_type=jnp.float32)  23.4 us
    dot_general x6, matrix products, one_head(): jnp.dot(selected, key_hot.T, preferred_element_type=jnp.float32) > 0.5  22.2 us
  transfers between devices with their start and end apart: 7, of which 4 were waited for; matrix products, arithmetic and copies ran while one was open for 37% of the time, Pallas kernels for 0%

commit v1 on v0

v1 whole, which is shorter than its diff:
```python
import functools
import math

import jax
import jax.numpy as jnp
from jax import lax
from jax.experimental import pallas as pl
from jax.experimental.pallas import tpu as pltpu
from jax.sharding import PartitionSpec as P

MESH = pl.DeviceIdType.MESH
HEAD_SIZE = 128
MASKED = -float(2**20)
CHUNK = 256

Q, LAB, K, V, O = range(5)


def iota(shape, dim):
    return lax.broadcasted_iota(jnp.int32, shape, dim)


def hot(mask):
    return jnp.where(mask, 1.0, 0.0).astype(jnp.bfloat16)


def dot_nt(a, b):
    return lax.dot_general(a, b, (((1,), (1,)), ((), ())), preferred_element_type=jnp.float32)


def dot_tn(a, b):
    return lax.dot_general(a, b, (((0,), (0,)), ((), ())), preferred_element_type=jnp.float32)


def relative_slots(label_ref, owner_rows, me, n, capacity, slot_ref):
    clusters = owner_rows.shape[1]
    upper = hot(iota((128, 128), 0) <= iota((128, 128), 1))
    seen = jnp.zeros((n, 1), jnp.float32)
    for start in range(0, label_ref.shape[1], 128):
        labels = label_ref[0:1, start : start + 128]
        cluster_hot = hot(iota((clusters, 128), 0) == labels)
        owner = jnp.dot(owner_rows, cluster_hot, preferred_element_type=jnp.float32)[0:1]
        relative = owner.astype(jnp.int32) - me
        relative = jnp.where(relative < 0, relative + n, relative)
        match = iota((n, 128), 0) == relative
        owner_hot = jnp.where(match, 1.0, 0.0)
        counts = jnp.dot(
            owner_hot.astype(jnp.bfloat16), upper, preferred_element_type=jnp.float32
        )
        rank = jnp.sum(jnp.where(match, counts + seen, 0.0), axis=0, keepdims=True) - 1.0
        slot_ref[0:1, start : start + 128] = relative * capacity + rank.astype(jnp.int32)
        seen = seen + jnp.sum(owner_hot, axis=1, keepdims=True)


def exchange_kernel(
    n, q_ref, k_ref, v_ref, qc_ref, kc_ref, owner_ref, bias_ref, out_ref,
    sq, rq, slab, rlab, sk, rk, sv, rv, so, ro, q_slot, k_slot, key_hot, probs, inverse,
    send_sem, recv_sem,
):
    me = lax.axis_index("seq")
    q_rows, k_rows = q_ref.shape[0], k_ref.shape[0]
    q_cap, k_cap = 2 * q_rows // n, 2 * k_rows // n
    heads, clusters = bias_ref.shape[0], bias_ref.shape[1]
    per_chunk = CHUNK // k_cap
    slots_q, slots_k = n * q_cap, n * k_cap

    def peer(i):
        return lax.rem(me + i, n)

    def copy(kind, i):
        source, target, rows = {
            Q: (sq, rq, q_cap), K: (sk, rk, k_cap), V: (sv, rv, k_cap),
            O: (so, ro, q_cap), LAB: (slab, rlab, 0),
        }[kind]
        if rows:
            window = pl.ds(pl.multiple_of(i * rows, rows), rows)
        else:
            window = i
        return pltpu.make_async_remote_copy(
            src_ref=source.at[window],
            dst_ref=target.at[window],
            send_sem=send_sem.at[kind, i],
            recv_sem=recv_sem.at[kind, i],
            device_id={"seq": peer(n - i) if kind == O else peer(i)},
            device_id_type=MESH,
        )

    barrier = pltpu.get_barrier_semaphore()

    @pl.loop(1, n)
    def _(i):
        pl.semaphore_signal(barrier, inc=1, device_id={"seq": peer(i)}, device_id_type=MESH)

    owner_rows = jnp.broadcast_to(
        owner_ref[...].astype(jnp.float32), (8, clusters)
    ).astype(jnp.bfloat16)
    relative_slots(qc_ref, owner_rows, me, n, q_cap, q_slot)
    relative_slots(kc_ref, owner_rows, me, n, k_cap, k_slot)

    pack_q = hot(iota((slots_q, q_rows), 0) == q_slot[...])
    sq[...] = jnp.dot(pack_q, q_ref[...], preferred_element_type=jnp.float32).astype(sq.dtype)
    q_labels = jnp.broadcast_to(
        (qc_ref[...] + 1).astype(jnp.float32), (8, q_rows)
    ).astype(jnp.bfloat16)
    packed = dot_nt(q_labels, pack_q)
    per_row = 128 // q_cap
    for i in range(n):
        group = i // per_row * 128
        slab[i, 1:2, :] = packed[0:1, group : group + 128]
    k_labels = jnp.broadcast_to(
        (kc_ref[...] + 1).astype(jnp.float32), (8, k_rows)
    ).astype(jnp.bfloat16)

    pl.semaphore_wait(barrier, n - 1)

    @pl.loop(0, slots_k // CHUNK)
    def _(j):
        base = pl.multiple_of(j * CHUNK, CHUNK)
        pack = hot(iota((CHUNK, k_rows), 0) + base == k_slot[...])
        sk[pl.ds(base, CHUNK), :] = jnp.dot(
            pack, k_ref[...], preferred_element_type=jnp.float32
        ).astype(sk.dtype)
        labels = dot_nt(k_labels, pack)
        for t in range(per_chunk):
            first = t * k_cap // 128 * 128
            slab[j * per_chunk + t, 0:1, :] = labels[0:1, first : first + 128]
        for t in range(per_chunk):
            i = j * per_chunk + t

            @pl.when(i > 0)
            def _():
                copy(LAB, i).start()
                copy(Q, i).start()
                copy(K, i).start()

    @pl.loop(0, slots_k // CHUNK)
    def _(j):
        base = pl.multiple_of(j * CHUNK, CHUNK)
        pack = hot(iota((CHUNK, k_rows), 0) + base == k_slot[...])
        sv[pl.ds(base, CHUNK), :] = jnp.dot(
            pack, v_ref[...], preferred_element_type=jnp.float32
        ).astype(sv.dtype)
        for t in range(per_chunk):
            i = j * per_chunk + t

            @pl.when(i > 0)
            def _():
                copy(V, i).start()

    rq[0:q_cap, :] = sq[0:q_cap, :]
    rk[0:k_cap, :] = sk[0:k_cap, :]
    rv[0:k_cap, :] = sv[0:k_cap, :]
    rlab[0] = slab[0]

    @pl.loop(1, n)
    def _(i):
        copy(LAB, i).wait_recv()
        copy(Q, i).wait_recv()
        copy(K, i).wait_recv()

    lane = iota((1, 128), 1)
    q_row = []
    for first in range(0, n, per_row):
        row = jnp.zeros((1, 128), jnp.float32)
        for i in range(first, first + per_row):
            row = jnp.where(lane // q_cap == i % per_row, rlab[i, 1:2, :], row)
        q_row.append(row)
    query_hot = [
        hot(iota((clusters, 128), 0) == row.astype(jnp.int32) - 1) for row in q_row
    ]
    query_hot = jnp.concatenate(query_hot, axis=1)
    per_lanes = 128 // k_cap
    for first in range(0, n, per_lanes):
        row = rlab[first, 0:1, :]
        for i in range(first + 1, first + per_lanes):
            row = jnp.where(lane // k_cap == i % per_lanes, rlab[i, 0:1, :], row)
        row = row.astype(jnp.int32) - 1
        key_hot[:, first * k_cap : first * k_cap + 128] = hot(
            (iota((clusters, 128), 0) == row) | (row < 0)
        )

    exponent = 1.0 / math.sqrt(HEAD_SIZE) / math.log(2.0)
    half = slots_q // 2

    def columns(h):
        return pl.ds(pl.multiple_of(h * HEAD_SIZE, HEAD_SIZE), HEAD_SIZE)

    @pl.loop(0, heads)
    def _(h):
        selected = dot_tn(query_hot, bias_ref[h]).astype(jnp.bfloat16)
        for part in range(2):
            rows = slice(part * half, (part + 1) * half)
            scores = dot_nt(rq[rows, columns(h)], rk[:, columns(h)])
            scores = scores + jnp.dot(
                selected[rows], key_hot[...], preferred_element_type=jnp.float32
            )
            largest = jnp.maximum(jnp.max(scores, axis=1, keepdims=True), 0.0)
            weights = jnp.exp2((scores - largest) * exponent)
            total = jnp.exp2(-largest * exponent) + jnp.sum(weights, axis=1, keepdims=True)
            probs[h, rows, :] = weights.astype(jnp.bfloat16)
            inverse[h, rows, :] = 1.0 / total

    @pl.loop(1, n)
    def _(i):
        copy(V, i).wait_recv()

    @pl.loop(0, heads)
    def _(h):
        so[:, columns(h)] = (
            jnp.dot(probs[h], rv[:, columns(h)], preferred_element_type=jnp.float32)
            * inverse[h]
        ).astype(so.dtype)

    @pl.loop(1, n)
    def _(i):
        copy(O, i).start()

    ro[0:q_cap, :] = so[0:q_cap, :]

    @pl.loop(1, n)
    def _(i):
        copy(O, i).wait_recv()

    unpack = hot(iota((slots_q, q_rows), 0) == q_slot[...])
    out_ref[...] = dot_tn(unpack, ro[...]).astype(out_ref.dtype)

    @pl.loop(1, n)
    def _(i):
        for kind in (LAB, Q, K, V, O):
            copy(kind, i).wait_send()


def attend(queries, keys, values, query_cluster, key_cluster, cluster_owner, bias):
    n = lax.axis_size("seq")
    q_rows, width = queries.shape
    k_rows = keys.shape[0]
    slots_q, slots_k = 2 * q_rows, 2 * k_rows
    heads, clusters = bias.shape[0], bias.shape[1]
    vmem = pl.BlockSpec(memory_space=pltpu.VMEM)

    def rows(count):
        return pltpu.VMEM((count, width), jnp.bfloat16)

    return pl.pallas_call(
        functools.partial(exchange_kernel, n),
        out_shape=jax.ShapeDtypeStruct((q_rows, width), jnp.bfloat16),
        in_specs=[vmem] * 7,
        out_specs=vmem,
        scratch_shapes=[
            rows(slots_q), rows(slots_q),
            pltpu.VMEM((n, 8, 128), jnp.float32), pltpu.VMEM((n, 8, 128), jnp.float32),
            rows(slots_k), rows(slots_k), rows(slots_k), rows(slots_k),
            rows(slots_q), rows(slots_q),
            pltpu.VMEM((1, q_rows), jnp.int32), pltpu.VMEM((1, k_rows), jnp.int32),
            pltpu.VMEM((clusters, slots_k), jnp.bfloat16),
            pltpu.VMEM((heads, slots_q, slots_k), jnp.bfloat16),
            pltpu.VMEM((heads, slots_q, 1), jnp.float32),
            pltpu.SemaphoreType.DMA((5, n)), pltpu.SemaphoreType.DMA((5, n)),
        ],
        compiler_params=pltpu.CompilerParams(
            collective_id=0, has_side_effects=True, vmem_limit_bytes=48 * 2**20
        ),
        cost_estimate=pl.CostEstimate(
            flops=2 * 10**11, bytes_accessed=16 * 2**20, transcendentals=0
        ),
    )(queries, keys, values, query_cluster[None], key_cluster[None], cluster_owner[None], bias)


def per_device(
    queries, keys, values, query_cluster, key_cluster, cluster_owner, pair_list, out_weight
):
    clusters = cluster_owner.shape[0]
    listed = jnp.any(
        pair_list[:, :, :, None] == jnp.arange(clusters, dtype=jnp.int32)[None, None, None, :],
        axis=2,
    )
    bias = jnp.where(listed, 0.0, MASKED).astype(jnp.bfloat16)
    attended = attend(
        queries, keys, values, query_cluster, key_cluster, cluster_owner, bias
    )
    terms = jnp.dot(
        attended,
        lax.all_gather(out_weight, "seq", axis=1, tiled=True),
        preferred_element_type=jnp.float32,
    )
    return lax.psum_scatter(terms, "head", scatter_dimension=1, tiled=True).astype(jnp.bfloat16)


def solution(mesh):
    in_specs = (
        P("seq", "head"),
        P("seq", "head"),
        P("seq", "head"),
        P("seq"),
        P("seq"),
        P(),
        P("head", None, None),
        P("head", "seq"),
    )
    out_specs = P("seq", "head")
    return jax.shard_map(
        per_device, mesh=mesh, in_specs=in_specs, out_specs=out_specs, check_vma=False
    )
```

time: 497 us -> 328 us (0.66)
  Pallas kernels: 0 us -> 250 us
  waiting for transfers between devices: 187 us -> 44.3 us
  local copies, waits for them, and re-layouts: 110 us -> 5.83 us
  matrix products: 72 us -> 11.5 us
  starting transfers between devices: 46.6 us -> 0.04 us
  other arithmetic: 38.7 us -> 2.96 us
  blocking collectives: 25.6 us -> 0 us
    pallas_call x0 -> x1, Pallas kernels: none -> 250 us  [attend(): pl.pallas_call(functools.partial(exchange_kernel, n), out_shape=jax.Shape...]
    all_to_all x5 -> x0, waiting for transfers between devices: 138 us -> none  [the longest x1 64.7 us: per_device(): lax.all_to_all(value_slots, 'seq', split_axis=0, concat_axis=0, tiled=True)]
    dot_general x18 -> x0, matrix products: 60.5 us -> none  [the longest x6 23.4 us: one_head(): jnp.dot(query_part, key_part.T, preferred_element_type=jnp.float32)]
    scatter x2 -> x0, local copies, waits for them, and re-layouts: 55.9 us -> none  [the longest x1 34.2 us: pack_rows(): return holder.at[owners, slot_rank].set(rows)]
    all_to_all x5 -> x0, starting transfers between devices: 46.5 us -> none  [the longest x1 11.9 us: per_device(): lax.all_to_all(query_labels, 'seq', split_axis=0, concat_axis=0, tiled=True)]
    unnamed x14 -> x12, local copies, waits for them, and re-layouts: 32 us -> 5.83 us
    all_to_all x1 -> x0, blocking collectives: 25.6 us -> none  [per_device(): lax.all_to_all(answered, 'seq', split_axis=0, concat_axis=0, tiled=True)]
    reduce_sum x10 -> x0, other arithmetic: 23.7 us -> none  [the longest x6 21.6 us: one_head(): total = jnp.exp(-largest) + jnp.sum(weights, axis=1)]
  transfers between devices with their start and end apart: 7 -> 2, of which waited for: 4 -> 1; matrix products, arithmetic and copies ran while one was open for 37% -> 0% of each run, Pallas kernels for 0% -> 76%
where the time goes in v1:
time: 328 us
  Pallas kernels  250 us (76%)
  waiting for transfers between devices  44.3 us (14%)
  between operations  13.4 us (4%)
  matrix products  11.5 us (4%)
  local copies, waits for them, and re-layouts  5.83 us (2%)
    pallas_call x1, Pallas kernels, attend(): pl.pallas_call(functools.partial(exchange_kernel, n), out_shape=jax.Shape...  250 us
    reduce_scatter x1, waiting for transfers between devices, per_device(): lax.psum_scatter(terms, 'head', scatter_dimension=1, tiled=True)  43.6 us
    dot_general x1, matrix products, per_device(): jnp.dot(attended, lax.all_gather(out_weight, 'seq', axis=1, tiled=True),...  11.5 us
  transfers between devices with their start and end apart: 2, of which 1 were waited for; matrix products, arithmetic and copies ran while one was open for 0% of the time, Pallas kernels for 76%

profile of v1, /device:TPU:1, one launch (start us, length us, event | category | flops | bytes accessed | tf_op | source)
XLA Modules:
  0.0 327.7 jit_solution(13028008205597703331)
XLA Ops:
  6.5 0.0 all-gather.2.cloned.1.call-start
  6.5 0.7 all-gather.2.cloned.1.call-update
  7.3 0.0 reduce-scatter.2.cloned.1.call-start
  7.3 1.0 fusion
  8.3 0.1 select_convert_fusion.bias_ref
  8.4 0.0 copy-start
  8.4 1.4 copy-done
  9.8 0.0 copy-start.1
  9.8 1.4 copy-done.1
  11.2 0.0 copy-start.2
  11.2 1.0 copy-done.2
  12.2 0.0 copy-start.3
  12.2 0.7 copy-done.3
  12.9 0.0 copy-start.4
  12.9 0.7 copy-done.4
  13.5 0.0 copy-start.5
  13.5 0.7 copy-done.5
  14.2 249.6 %shard_map.82 = bf16[256,768]{1,0:T(8,128)(2,1)S(1)} custom-call(bf16[256,768]{1,0:T(8,128)(2,1)S(1)} %copy-done.2, bf16[1024,768]{1,0:T(8,128)(2,1)S(1)} %copy-done, bf16[1024,768]{1,0:T(8,128)(2,1)S(1)} %copy-done.1, s32[1,256]{1,0:T(1,128)S(1)} %bitcast.6, s32[1,1024]{1,0:T(1,128)S(1)} %bitcast.5, s32[1,128]{1,0:T(1,128)S(1)} %bitcast.7, ...), custom_call_target="tpu_custom_call" | custom-call | flops 199999995904 | bytes 16777216 | tf_op jit(solution)/shard_map/pallas_call | solution.py:244
  263.8 0.0 all-gather.2.cloned.1.call-done
  263.8 11.5 %fusion.1 = f32[256,6144]{1,0:T(8,128)} fusion(bf16[256,768]{1,0:T(8,128)(2,1)S(1)} %shard_map.82, bf16[768,6144]{0,1:T(8,128)(2,1)} %all-gather.2.cloned.1.call-done), kind=kOutput, calls=%fused_computation.3 | convolution fusion | flops 2415919104 | bytes 16121856 | tf_op jit(solution)/shard_map/dot_general | solution.py:281
  275.4 0.0 reduce-scatter.2.cloned.1.call-update
  275.4 43.6 %reduce-scatter.2.cloned.1.call-done = f32[256,768]{1,0:T(8,128)} async-done(((f32[256,6144]{1,0:T(8,128)}), f32[256,768]{1,0:T(8,128)}) %reduce-scatter.2.cloned.1.call-update) | async-done | bytes 786448 | tf_op jit(solution)/shard_map/reduce_scatter | solution.py:286
  318.9 1.9 convert_element_type.7
Async XLA Ops:
  6.5 257.3 %all-gather.2.cloned.1.call-start = ((), (), s32[]{:S(2)}) async-start(), calls=%async_computation.1 | async-start | bytes 9732096 | tf_op jit(solution)/shard_map/all_gather | solution.py:283
  7.3 311.7 %reduce-scatter.2.cloned.1.call-start = ((), (), s32[]{:S(2)}) async-start(), calls=%async_computation.2 | async-start | bytes 7077888 | tf_op jit(solution)/shard_map/reduce_scatter | solution.py:286
  8.4 1.4 copy-start
  9.8 1.4 copy-start.1
  11.2 1.0 copy-start.2
  12.2 0.7 copy-start.3
  12.9 0.7 copy-start.4
  13.5 0.7 copy-start.5
Sparse Core Ops, SparseCore 0:
  9.9 227.1 all-gather.1
  275.5 43.3 reduce-scatter.1

commit v2 on v1

--- a/solution.py
+++ b/solution.py
@@ -14,6 +14,7 @@
 CHUNK = 256
 
 Q, LAB, K, V, O = range(5)
+X_SIZE = 4
 
 
 def iota(shape, dim):
@@ -30,6 +31,21 @@
 
 def dot_tn(a, b):
     return lax.dot_general(a, b, (((0,), (0,)), ((), ())), preferred_element_type=jnp.float32)
+
+
+def offset(i, n):
+    z_size = n // X_SIZE
+    a, k = i // z_size, lax.rem(i, z_size)
+    dz = (k + 1) // 2 * (2 * lax.rem(k, 2) - 1)
+    return lax.rem(a + k, X_SIZE), dz
+
+
+def order_of(owner, me, n):
+    z_size = n // X_SIZE
+    dx = (owner // z_size - me // z_size) & (X_SIZE - 1)
+    dz = (owner - me) & (z_size - 1)
+    k = jnp.where(dz <= z_size // 2, jnp.maximum(2 * dz - 1, 0), 2 * (z_size - dz))
+    return ((dx - k) & (X_SIZE - 1)) * z_size + k
 
 
 def relative_slots(label_ref, owner_rows, me, n, capacity, slot_ref):
@@ -40,8 +56,7 @@
         labels = label_ref[0:1, start : start + 128]
         cluster_hot = hot(iota((clusters, 128), 0) == labels)
         owner = jnp.dot(owner_rows, cluster_hot, preferred_element_type=jnp.float32)[0:1]
-        relative = owner.astype(jnp.int32) - me
-        relative = jnp.where(relative < 0, relative + n, relative)
+        relative = order_of(owner.astype(jnp.int32), me, n)
         match = iota((n, 128), 0) == relative
         owner_hot = jnp.where(match, 1.0, 0.0)
         counts = jnp.dot(
@@ -53,19 +68,29 @@
 
 
 def exchange_kernel(
-    n, q_ref, k_ref, v_ref, qc_ref, kc_ref, owner_ref, bias_ref, out_ref,
-    sq, rq, slab, rlab, sk, rk, sv, rv, so, ro, q_slot, k_slot, key_hot, probs, inverse,
-    send_sem, recv_sem,
+    n, n_head, q_ref, k_ref, v_ref, w_ref, qc_ref, kc_ref, owner_ref, bias_ref, out_ref,
+    sq, rq, slab, rlab, sk, rk, sv, rv, so, ro, q_slot, k_slot, key_hot, probs,
+    pieces, weight, mixed_in,
+    send_sem, recv_sem, piece_send, piece_recv, w_send, w_recv, a_send, a_recv,
 ):
     me = lax.axis_index("seq")
+    head = lax.axis_index("head")
+    parts = n // n_head
+    depth = w_ref.shape[0] // parts
+    z_size = n // X_SIZE
+    x, z = me // z_size, lax.rem(me, z_size)
     q_rows, k_rows = q_ref.shape[0], k_ref.shape[0]
     q_cap, k_cap = 2 * q_rows // n, 2 * k_rows // n
     heads, clusters = bias_ref.shape[0], bias_ref.shape[1]
     per_chunk = CHUNK // k_cap
     slots_q, slots_k = n * q_cap, n * k_cap
 
-    def peer(i):
-        return lax.rem(me + i, n)
+    def at(dx, dz):
+        return lax.rem(x + dx + X_SIZE, X_SIZE) * z_size + lax.rem(z + dz + z_size, z_size)
+
+    def peer(i, sign=1):
+        dx, dz = offset(i, n)
+        return at(sign * dx, sign * dz)
 
     def copy(kind, i):
         source, target, rows = {
@@ -81,11 +106,92 @@
             dst_ref=target.at[window],
             send_sem=send_sem.at[kind, i],
             recv_sem=recv_sem.at[kind, i],
-            device_id={"seq": peer(n - i) if kind == O else peer(i)},
+            device_id={"seq": peer(i, -1) if kind == O else peer(i)},
             device_id_type=MESH,
         )
 
+    here = me // parts == head
+
+    def piece_copy(j):
+        return pltpu.make_async_remote_copy(
+            src_ref=w_ref.at[pl.ds(j * depth, depth)],
+            dst_ref=pieces.at[lax.rem(me, parts)],
+            send_sem=piece_send.at[j],
+            recv_sem=piece_recv.at[lax.rem(me, parts)],
+            device_id={"seq": parts * head + j, "head": me // parts},
+            device_id_type=MESH,
+        )
+
+    def piece_stays(j):
+        return here & (lax.rem(me, parts) == j)
+
+    def piece_local(j):
+        return pltpu.make_async_copy(
+            w_ref.at[pl.ds(j * depth, depth)], pieces.at[j], piece_recv.at[j]
+        )
+
+    def weight_copy(block, target, index):
+        window = pl.ds(pl.multiple_of(block * depth, depth), depth)
+        return pltpu.make_async_remote_copy(
+            src_ref=weight.at[window],
+            dst_ref=weight.at[window],
+            send_sem=w_send.at[index],
+            recv_sem=w_recv.at[block],
+            device_id={"seq": target},
+            device_id_type=MESH,
+        )
+
+    far = z_size // 2
+    z_first = [(0, 1), (0, -1), (0, far)]
+    z_second = [(-1, 1), (1, -1), (far, 1), (far, -1)]
+
+    def z_first_copy(i):
+        return weight_copy(me, at(0, z_first[i][1]), i)
+
+    def z_second_copy(i):
+        return weight_copy(at(0, z_second[i][0]), at(0, z_second[i][1]), 3 + i)
+
+    def x_first_copy(dz, i):
+        return weight_copy(at(0, dz), at(1 - 2 * i, 0), 7 + 2 * (dz % z_size) + i)
+
+    def x_second_copy(dz):
+        step = 1 - 2 * (dz % 2)
+        return weight_copy(at(-step, dz), at(step, 0), 7 + 2 * z_size + dz % z_size)
+
+    def wait_block(block):
+        weight_copy(block, me, 0).wait_recv()
+
+    z_near = [0, 1, -1, far]
+    z_later = [2, -2, 3, -3]
+
+    mate = head + 1 - 2 * lax.rem(head, 2)
+
+    def along(t):
+        return lax.rem(head + 2 * t, n_head)
+
+    def block_copy(block, target, index):
+        return pltpu.make_async_remote_copy(
+            src_ref=mixed_in.at[block],
+            dst_ref=mixed_in.at[block],
+            send_sem=a_send.at[index],
+            recv_sem=a_recv.at[block],
+            device_id={"head": target},
+            device_id_type=MESH,
+        )
+
     barrier = pltpu.get_barrier_semaphore()
+    ys = n_head // 2
+    for t in range(1, ys):
+        pl.semaphore_signal(barrier, inc=1, device_id={"head": along(t)}, device_id_type=MESH)
+    pl.semaphore_signal(barrier, inc=1, device_id={"head": mate}, device_id_type=MESH)
+    for j in range(parts):
+
+        @pl.when(jnp.logical_not(piece_stays(j)))
+        def _():
+            pl.semaphore_signal(
+                barrier, inc=1, device_id={"seq": parts * head + j, "head": me // parts},
+                device_id_type=MESH,
+            )
 
     @pl.loop(1, n)
     def _(i):
@@ -111,7 +217,23 @@
         (kc_ref[...] + 1).astype(jnp.float32), (8, k_rows)
     ).astype(jnp.bfloat16)
 
-    pl.semaphore_wait(barrier, n - 1)
+    @pl.when(here)
+    def _():
+        pl.semaphore_wait(barrier, n - 1 + ys + parts - 1)
+
+    @pl.when(jnp.logical_not(here))
+    def _():
+        pl.semaphore_wait(barrier, n - 1 + ys + parts)
+
+    for j in range(parts):
+
+        @pl.when(piece_stays(j))
+        def _():
+            piece_local(j).start()
+
+        @pl.when(jnp.logical_not(piece_stays(j)))
+        def _():
+            piece_copy(j).start()
 
     @pl.loop(0, slots_k // CHUNK)
     def _(j):
@@ -133,19 +255,44 @@
                 copy(Q, i).start()
                 copy(K, i).start()
 
-    @pl.loop(0, slots_k // CHUNK)
-    def _(j):
-        base = pl.multiple_of(j * CHUNK, CHUNK)
-        pack = hot(iota((CHUNK, k_rows), 0) + base == k_slot[...])
-        sv[pl.ds(base, CHUNK), :] = jnp.dot(
-            pack, v_ref[...], preferred_element_type=jnp.float32
-        ).astype(sv.dtype)
-        for t in range(per_chunk):
-            i = j * per_chunk + t
-
-            @pl.when(i > 0)
-            def _():
-                copy(V, i).start()
+    for j in range(parts):
+        piece_local(j).wait()
+    weight[pl.ds(pl.multiple_of(me * depth, depth), depth), :] = jnp.concatenate(
+        [pieces[j] for j in range(parts)], axis=1
+    )
+    for i in range(3):
+        z_first_copy(i).start()
+
+    def send_values(first, last):
+        @pl.loop(first, last)
+        def _(j):
+            base = pl.multiple_of(j * CHUNK, CHUNK)
+            pack = hot(iota((CHUNK, k_rows), 0) + base == k_slot[...])
+            sv[pl.ds(base, CHUNK), :] = jnp.dot(
+                pack, v_ref[...], preferred_element_type=jnp.float32
+            ).astype(sv.dtype)
+            for t in range(per_chunk):
+                i = j * per_chunk + t
+
+                @pl.when(i > 0)
+                def _():
+                    copy(V, i).start()
+
+    chunks = slots_k // CHUNK
+    send_values(0, chunks // 2)
+    for dz in (1, -1, far):
+        wait_block(at(0, dz))
+    for i in range(4):
+        z_second_copy(i).start()
+    for dz in z_near:
+        for i in range(2):
+            x_first_copy(dz, i).start()
+    send_values(chunks // 2, chunks)
+    for dz in z_later:
+        wait_block(at(0, dz))
+    for dz in z_later:
+        for i in range(2):
+            x_first_copy(dz, i).start()
 
     rq[0:q_cap, :] = sq[0:q_cap, :]
     rk[0:k_cap, :] = sk[0:k_cap, :]
@@ -197,8 +344,12 @@
             largest = jnp.maximum(jnp.max(scores, axis=1, keepdims=True), 0.0)
             weights = jnp.exp2((scores - largest) * exponent)
             total = jnp.exp2(-largest * exponent) + jnp.sum(weights, axis=1, keepdims=True)
-            probs[h, rows, :] = weights.astype(jnp.bfloat16)
-            inverse[h, rows, :] = 1.0 / total
+            probs[h, rows, :] = (weights * (1.0 / total)).astype(jnp.bfloat16)
+
+    for dz in z_near + z_later:
+        wait_block(at(1, dz))
+        wait_block(at(-1, dz))
+        x_second_copy(dz).start()
 
     @pl.loop(1, n)
     def _(i):
@@ -206,9 +357,8 @@
 
     @pl.loop(0, heads)
     def _(h):
-        so[:, columns(h)] = (
-            jnp.dot(probs[h], rv[:, columns(h)], preferred_element_type=jnp.float32)
-            * inverse[h]
+        so[:, columns(h)] = jnp.dot(
+            probs[h], rv[:, columns(h)], preferred_element_type=jnp.float32
         ).astype(so.dtype)
 
     @pl.loop(1, n)
@@ -222,16 +372,61 @@
         copy(O, i).wait_recv()
 
     unpack = hot(iota((slots_q, q_rows), 0) == q_slot[...])
-    out_ref[...] = dot_tn(unpack, ro[...]).astype(out_ref.dtype)
+    mixed_in[head] = dot_tn(unpack, ro[...]).astype(mixed_in.dtype)
+    for t in range(1, ys):
+        block_copy(head, along(t), t - 1).start()
+    block_copy(head, mate, ys - 1).start()
+
+    for dz in z_near + z_later:
+        wait_block(at(2, dz))
+
+    def product(block):
+        width = mixed_in.shape[2]
+        return jnp.dot(
+            mixed_in[block], weight[pl.ds(pl.multiple_of(block * width, width), width), :],
+            preferred_element_type=jnp.float32,
+        )
+
+    total = product(head)
+    for t in range(1, ys):
+        block_copy(along(t), mate, 0).wait_recv()
+        block_copy(along(t), mate, ys - 1 + t).start()
+        total = total + product(along(t))
+    for t in range(ys):
+        block = lax.rem(mate + 2 * t, n_head)
+        block_copy(block, mate, 0).wait_recv()
+        total = total + product(block)
+    out_ref[...] = total.astype(out_ref.dtype)
 
     @pl.loop(1, n)
     def _(i):
         for kind in (LAB, Q, K, V, O):
             copy(kind, i).wait_send()
 
-
-def attend(queries, keys, values, query_cluster, key_cluster, cluster_owner, bias):
-    n = lax.axis_size("seq")
+    for j in range(parts):
+
+        @pl.when(jnp.logical_not(piece_stays(j)))
+        def _():
+            piece_copy(j).wait_send()
+
+    for i in range(3):
+        z_first_copy(i).wait_send()
+    for i in range(4):
+        z_second_copy(i).wait_send()
+    for dz in range(z_size):
+        for i in range(2):
+            x_first_copy(dz, i).wait_send()
+        x_second_copy(dz).wait_send()
+    for t in range(1, ys):
+        block_copy(head, along(t), t - 1).wait_send()
+        block_copy(along(t), mate, ys - 1 + t).wait_send()
+    block_copy(head, mate, ys - 1).wait_send()
+
+
+def mix(queries, keys, values, out_weight, query_cluster, key_cluster, cluster_owner, bias):
+    n, n_head = lax.axis_size("seq"), lax.axis_size("head")
+    parts = n // n_head
+    depth, narrow = out_weight.shape[0] // parts, out_weight.shape[1]
     q_rows, width = queries.shape
     k_rows = keys.shape[0]
     slots_q, slots_k = 2 * q_rows, 2 * k_rows
@@ -242,9 +437,9 @@
         return pltpu.VMEM((count, width), jnp.bfloat16)
 
     return pl.pallas_call(
-        functools.partial(exchange_kernel, n),
-        out_shape=jax.ShapeDtypeStruct((q_rows, width), jnp.bfloat16),
-        in_specs=[vmem] * 7,
+        functools.partial(exchange_kernel, n, n_head),
+        out_shape=jax.ShapeDtypeStruct((q_rows, narrow * parts), jnp.bfloat16),
+        in_specs=[vmem] * 8,
         out_specs=vmem,
         scratch_shapes=[
             rows(slots_q), rows(slots_q),
@@ -254,16 +449,24 @@
             pltpu.VMEM((1, q_rows), jnp.int32), pltpu.VMEM((1, k_rows), jnp.int32),
             pltpu.VMEM((clusters, slots_k), jnp.bfloat16),
             pltpu.VMEM((heads, slots_q, slots_k), jnp.bfloat16),
-            pltpu.VMEM((heads, slots_q, 1), jnp.float32),
+            pltpu.VMEM((parts, depth, narrow), jnp.bfloat16),
+            pltpu.VMEM((depth * n, narrow * parts), jnp.bfloat16),
+            pltpu.VMEM((n_head, q_rows, width), jnp.bfloat16),
             pltpu.SemaphoreType.DMA((5, n)), pltpu.SemaphoreType.DMA((5, n)),
+            pltpu.SemaphoreType.DMA((parts,)), pltpu.SemaphoreType.DMA((parts,)),
+            pltpu.SemaphoreType.DMA((n + 7,)), pltpu.SemaphoreType.DMA((n,)),
+            pltpu.SemaphoreType.DMA((n_head,)), pltpu.SemaphoreType.DMA((n_head,)),
         ],
         compiler_params=pltpu.CompilerParams(
-            collective_id=0, has_side_effects=True, vmem_limit_bytes=48 * 2**20
+            collective_id=0, has_side_effects=True, vmem_limit_bytes=60 * 2**20
         ),
         cost_estimate=pl.CostEstimate(
             flops=2 * 10**11, bytes_accessed=16 * 2**20, transcendentals=0
         ),
-    )(queries, keys, values, query_cluster[None], key_cluster[None], cluster_owner[None], bias)
+    )(
+        queries, keys, values, out_weight, query_cluster[None], key_cluster[None],
+        cluster_owner[None], bias,
+    )
 
 
 def per_device(
@@ -275,15 +478,9 @@
         axis=2,
     )
     bias = jnp.where(listed, 0.0, MASKED).astype(jnp.bfloat16)
-    attended = attend(
-        queries, keys, values, query_cluster, key_cluster, cluster_owner, bias
+    return mix(
+        queries, keys, values, out_weight, query_cluster, key_cluster, cluster_owner, bias
     )
-    terms = jnp.dot(
-        attended,
-        lax.all_gather(out_weight, "seq", axis=1, tiled=True),
-        preferred_element_type=jnp.float32,
-    )
-    return lax.psum_scatter(terms, "head", scatter_dimension=1, tiled=True).astype(jnp.bfloat16)
 
 
 def solution(mesh):

time: 328 us -> 294 us (0.90)
  waiting for transfers between devices: 44.3 us -> 0 us
  Pallas kernels: 250 us -> 288 us
  between operations: 13.4 us -> 0.02 us
  matrix products: 11.5 us -> 0 us
    reduce_scatter x1 -> x0, waiting for transfers between devices: 43.6 us -> none  [per_device(): lax.psum_scatter(terms, 'head', scatter_dimension=1, tiled=True)]
    pallas_call x1, Pallas kernels: 250 us -> 288 us  [mix(): pl.pallas_call(functools.partial(exchange_kernel, n, n_head), out_shape=j...]
    dot_general x1 -> x0, matrix products: 11.5 us -> none  [per_device(): jnp.dot(attended, lax.all_gather(out_weight, 'seq', axis=1, tiled=True),...]
  transfers between devices with their start and end apart: 2 -> 0, of which waited for: 1 -> 0; matrix products, arithmetic and copies ran while one was open for 0% -> 0% of each run, Pallas kernels for 76% -> 0%
where the time goes in v2:
time: 294 us; the launch traced here: 293 us
  Pallas kernels  288 us (98%)
  local copies, waits for them, and re-layouts  3.65 us (1%)
    pallas_call x1, Pallas kernels, mix(): pl.pallas_call(functools.partial(exchange_kernel, n, n_head), out_shape=j...  288 us

profile of v2, /device:TPU:1, one launch (start us, length us, event | category | flops | bytes accessed | tf_op | source)
XLA Modules:
  0.0 293.5 jit_solution(4184619705911803608)
XLA Ops:
  0.0 1.0 fusion
  1.0 0.7 select_convert_fusion.bias_ref
  1.7 1.9 copy.11.w_ref
  3.6 288.1 %shard_map.82 = bf16[256,768]{1,0:T(8,128)(2,1)} custom-call(bf16[256,768]{1,0:T(8,128)(2,1)} %q_ref.1, bf16[1024,768]{1,0:T(8,128)(2,1)} %k_ref.1, bf16[1024,768]{1,0:T(8,128)(2,1)} %v_ref.1, bf16[768,192]{1,0:T(8,128)(2,1)} %copy.11.w_ref, s32[1,256]{1,0:T(1,128)} %bitcast.4, s32[1,1024]{1,0:T(1,128)} %bitcast.3, s32[1,128]{1,0:T(1,128)} %bitcast.5, ...), custom_call_target="tpu_custom_call" | custom-call | flops 199999995904 | bytes 16777216 | tf_op jit(solution)/shard_map/pallas_call | solution.py:439
  291.7 1.8 copy.13

commit v3 on v2

--- a/solution.py
+++ b/solution.py
@@ -40,15 +40,15 @@
     return lax.rem(a + k, X_SIZE), dz
 
 
-def order_of(owner, me, n):
+def order_of(owner, me, n, sign):
     z_size = n // X_SIZE
-    dx = (owner // z_size - me // z_size) & (X_SIZE - 1)
-    dz = (owner - me) & (z_size - 1)
+    dx = sign * (owner // z_size - me // z_size) & (X_SIZE - 1)
+    dz = sign * (owner - me) & (z_size - 1)
     k = jnp.where(dz <= z_size // 2, jnp.maximum(2 * dz - 1, 0), 2 * (z_size - dz))
     return ((dx - k) & (X_SIZE - 1)) * z_size + k
 
 
-def relative_slots(label_ref, owner_rows, me, n, capacity, slot_ref):
+def relative_slots(label_ref, owner_rows, me, n, sign, capacity, slot_ref):
     clusters = owner_rows.shape[1]
     upper = hot(iota((128, 128), 0) <= iota((128, 128), 1))
     seen = jnp.zeros((n, 1), jnp.float32)
@@ -56,7 +56,7 @@
         labels = label_ref[0:1, start : start + 128]
         cluster_hot = hot(iota((clusters, 128), 0) == labels)
         owner = jnp.dot(owner_rows, cluster_hot, preferred_element_type=jnp.float32)[0:1]
-        relative = order_of(owner.astype(jnp.int32), me, n)
+        relative = order_of(owner.astype(jnp.int32), me, n, sign)
         match = iota((n, 128), 0) == relative
         owner_hot = jnp.where(match, 1.0, 0.0)
         counts = jnp.dot(
@@ -88,25 +88,25 @@
     def at(dx, dz):
         return lax.rem(x + dx + X_SIZE, X_SIZE) * z_size + lax.rem(z + dz + z_size, z_size)
 
-    def peer(i, sign=1):
+    mirror = 1 - 2 * lax.rem(head, 2)
+
+    def peer(i, back=1):
         dx, dz = offset(i, n)
-        return at(sign * dx, sign * dz)
+        return at(back * mirror * dx, back * mirror * dz)
 
     def copy(kind, i):
+        returning = kind >= O
         source, target, rows = {
-            Q: (sq, rq, q_cap), K: (sk, rk, k_cap), V: (sv, rv, k_cap),
-            O: (so, ro, q_cap), LAB: (slab, rlab, 0),
-        }[kind]
-        if rows:
-            window = pl.ds(pl.multiple_of(i * rows, rows), rows)
-        else:
-            window = i
+            Q: (sq, rq, q_cap), K: (sk, rk, k_cap), V: (sv, rv, k_cap), LAB: (slab, rlab, 0),
+        }.get(kind, (so, ro, q_cap))
+        first = (kind - O) * slots_q if returning else 0
+        window = pl.ds(pl.multiple_of(first + i * rows, rows), rows) if rows else i
         return pltpu.make_async_remote_copy(
             src_ref=source.at[window],
             dst_ref=target.at[window],
             send_sem=send_sem.at[kind, i],
             recv_sem=recv_sem.at[kind, i],
-            device_id={"seq": peer(i, -1) if kind == O else peer(i)},
+            device_id={"seq": peer(i, -1) if returning else peer(i)},
             device_id_type=MESH,
         )
 
@@ -130,51 +130,71 @@
             w_ref.at[pl.ds(j * depth, depth)], pieces.at[j], piece_recv.at[j]
         )
 
-    def weight_copy(block, target, index):
-        window = pl.ds(pl.multiple_of(block * depth, depth), depth)
+    def weight_copy(block, target, index, first=0, rows=None, arrival=None):
+        rows = rows or depth
+        window = pl.ds(pl.multiple_of(block * depth + first, rows), rows)
         return pltpu.make_async_remote_copy(
             src_ref=weight.at[window],
             dst_ref=weight.at[window],
             send_sem=w_send.at[index],
-            recv_sem=w_recv.at[block],
+            recv_sem=w_recv.at[block if arrival is None else arrival],
             device_id={"seq": target},
             device_id_type=MESH,
         )
 
     far = z_size // 2
-    z_first = [(0, 1), (0, -1), (0, far)]
-    z_second = [(-1, 1), (1, -1), (far, 1), (far, -1)]
-
-    def z_first_copy(i):
-        return weight_copy(me, at(0, z_first[i][1]), i)
-
-    def z_second_copy(i):
-        return weight_copy(at(0, z_second[i][0]), at(0, z_second[i][1]), 3 + i)
+
+    def z_copy(distance, way):
+        block, target = at(0, way * (1 - distance)), at(0, way)
+        index = 2 * (distance - 1) + (1 - way) // 2
+        if distance < far:
+            return weight_copy(block, target, index)
+        return weight_copy(block, target, index, *far_half(way))
+
+    def far_half(way):
+        return (0, depth // 2, None) if way > 0 else (depth // 2, depth // 2, n)
+
+    def wait_z(distance):
+        for way in (1, -1):
+            half = far_half(way) if distance == far else ()
+            weight_copy(at(0, -way * distance), me, 0, *half).wait_recv()
 
     def x_first_copy(dz, i):
-        return weight_copy(at(0, dz), at(1 - 2 * i, 0), 7 + 2 * (dz % z_size) + i)
+        return weight_copy(at(0, dz), at(1 - 2 * i, 0), z_size + 2 * (dz % z_size) + i)
 
     def x_second_copy(dz):
         step = 1 - 2 * (dz % 2)
-        return weight_copy(at(-step, dz), at(step, 0), 7 + 2 * z_size + dz % z_size)
+        return weight_copy(at(-step, dz), at(step, 0), 3 * z_size + dz % z_size)
 
     def wait_block(block):
         weight_copy(block, me, 0).wait_recv()
 
-    z_near = [0, 1, -1, far]
-    z_later = [2, -2, 3, -3]
+    def ring_step(distance):
+        wait_z(distance)
+        blocks = (far,) if distance == far else (distance, -distance)
+        if distance < far:
+            for way in (1, -1):
+                z_copy(distance + 1, way).start()
+        for dz in blocks:
+            for i in range(2):
+                x_first_copy(dz, i).start()
+
+    def x_step(dz):
+        wait_block(at(1, dz))
+        wait_block(at(-1, dz))
+        x_second_copy(dz).start()
 
     mate = head + 1 - 2 * lax.rem(head, 2)
 
     def along(t):
         return lax.rem(head + 2 * t, n_head)
 
-    def block_copy(block, target, index):
+    def block_copy(part, block, target, index):
         return pltpu.make_async_remote_copy(
-            src_ref=mixed_in.at[block],
-            dst_ref=mixed_in.at[block],
-            send_sem=a_send.at[index],
-            recv_sem=a_recv.at[block],
+            src_ref=mixed_in.at[block, part],
+            dst_ref=mixed_in.at[block, part],
+            send_sem=a_send.at[part, index],
+            recv_sem=a_recv.at[part, block],
             device_id={"head": target},
             device_id_type=MESH,
         )
@@ -200,8 +220,8 @@
     owner_rows = jnp.broadcast_to(
         owner_ref[...].astype(jnp.float32), (8, clusters)
     ).astype(jnp.bfloat16)
-    relative_slots(qc_ref, owner_rows, me, n, q_cap, q_slot)
-    relative_slots(kc_ref, owner_rows, me, n, k_cap, k_slot)
+    relative_slots(qc_ref, owner_rows, me, n, mirror, q_cap, q_slot)
+    relative_slots(kc_ref, owner_rows, me, n, mirror, k_cap, k_slot)
 
     pack_q = hot(iota((slots_q, q_rows), 0) == q_slot[...])
     sq[...] = jnp.dot(pack_q, q_ref[...], preferred_element_type=jnp.float32).astype(sq.dtype)
@@ -260,39 +280,34 @@
     weight[pl.ds(pl.multiple_of(me * depth, depth), depth), :] = jnp.concatenate(
         [pieces[j] for j in range(parts)], axis=1
     )
-    for i in range(3):
-        z_first_copy(i).start()
-
-    def send_values(first, last):
-        @pl.loop(first, last)
-        def _(j):
-            base = pl.multiple_of(j * CHUNK, CHUNK)
-            pack = hot(iota((CHUNK, k_rows), 0) + base == k_slot[...])
-            sv[pl.ds(base, CHUNK), :] = jnp.dot(
-                pack, v_ref[...], preferred_element_type=jnp.float32
-            ).astype(sv.dtype)
-            for t in range(per_chunk):
-                i = j * per_chunk + t
-
-                @pl.when(i > 0)
-                def _():
-                    copy(V, i).start()
+    for way in (1, -1):
+        z_copy(1, way).start()
+    for i in range(2):
+        x_first_copy(0, i).start()
 
     chunks = slots_k // CHUNK
-    send_values(0, chunks // 2)
-    for dz in (1, -1, far):
-        wait_block(at(0, dz))
-    for i in range(4):
-        z_second_copy(i).start()
-    for dz in z_near:
-        for i in range(2):
-            x_first_copy(dz, i).start()
-    send_values(chunks // 2, chunks)
-    for dz in z_later:
-        wait_block(at(0, dz))
-    for dz in z_later:
-        for i in range(2):
-            x_first_copy(dz, i).start()
+
+    @pl.loop(0, chunks)
+    def _(j):
+        base = pl.multiple_of(j * CHUNK, CHUNK)
+        pack = hot(iota((CHUNK, k_rows), 0) + base == k_slot[...])
+        sv[pl.ds(base, CHUNK), :] = jnp.dot(
+            pack, v_ref[...], preferred_element_type=jnp.float32
+        ).astype(sv.dtype)
+        for t in range(per_chunk):
+            i = j * per_chunk + t
+
+            @pl.when(i > 0)
+            def _():
+                copy(V, i).start()
+
+        for distance in range(1, far):
+
+            @pl.when(j == chunks * distance // far)
+            def _():
+                ring_step(distance)
+
+    ring_step(far)
 
     rq[0:q_cap, :] = sq[0:q_cap, :]
     rk[0:k_cap, :] = sk[0:k_cap, :]
@@ -346,61 +361,72 @@
             total = jnp.exp2(-largest * exponent) + jnp.sum(weights, axis=1, keepdims=True)
             probs[h, rows, :] = (weights * (1.0 / total)).astype(jnp.bfloat16)
 
-    for dz in z_near + z_later:
-        wait_block(at(1, dz))
-        wait_block(at(-1, dz))
-        x_second_copy(dz).start()
+    for dz in (0, 1, -1, 2, -2):
+        x_step(dz)
 
     @pl.loop(1, n)
     def _(i):
         copy(V, i).wait_recv()
 
-    @pl.loop(0, heads)
-    def _(h):
-        so[:, columns(h)] = jnp.dot(
-            probs[h], rv[:, columns(h)], preferred_element_type=jnp.float32
-        ).astype(so.dtype)
+    for part in range(2):
+
+        @pl.loop(0, heads // 2)
+        def _(h):
+            g = h + part * (heads // 2)
+            so[part * slots_q : (part + 1) * slots_q, columns(h)] = jnp.dot(
+                probs[g], rv[:, columns(g)], preferred_element_type=jnp.float32
+            ).astype(so.dtype)
+
+        @pl.loop(1, n)
+        def _(i):
+            copy(O + part, i).start()
+
+        own = slice(part * slots_q, part * slots_q + q_cap)
+        ro[own, :] = so[own, :]
+
+    for dz in (3, -3, far):
+        x_step(dz)
+
+    unpack = hot(iota((slots_q, q_rows), 0) == q_slot[...])
+    for part in range(2):
+
+        @pl.loop(1, n)
+        def _(i):
+            copy(O + part, i).wait_recv()
+
+        mixed_in[head, part] = dot_tn(
+            unpack, ro[part * slots_q : (part + 1) * slots_q, :]
+        ).astype(mixed_in.dtype)
+        for t in range(1, ys):
+            block_copy(part, head, along(t), t - 1).start()
+        block_copy(part, head, mate, ys - 1).start()
+
+    for dz in range(z_size):
+        wait_block(at(2, dz))
+
+    def product(part, block):
+        width = mixed_in.shape[3]
+        rows = pl.ds(pl.multiple_of((2 * block + part) * width, width), width)
+        return jnp.dot(
+            mixed_in[block, part], weight[rows, :], preferred_element_type=jnp.float32
+        )
+
+    total = product(0, head) + product(1, head)
+    for part in range(2):
+        for t in range(1, ys):
+            block_copy(part, along(t), mate, 0).wait_recv()
+            block_copy(part, along(t), mate, ys - 1 + t).start()
+            total = total + product(part, along(t))
+    for part in range(2):
+        for t in range(ys):
+            block = lax.rem(mate + 2 * t, n_head)
+            block_copy(part, block, mate, 0).wait_recv()
+            total = total + product(part, block)
+    out_ref[...] = total.astype(out_ref.dtype)
 
     @pl.loop(1, n)
     def _(i):
-        copy(O, i).start()
-
-    ro[0:q_cap, :] = so[0:q_cap, :]
-
-    @pl.loop(1, n)
-    def _(i):
-        copy(O, i).wait_recv()
-
-    unpack = hot(iota((slots_q, q_rows), 0) == q_slot[...])
-    mixed_in[head] = dot_tn(unpack, ro[...]).astype(mixed_in.dtype)
-    for t in range(1, ys):
-        block_copy(head, along(t), t - 1).start()
-    block_copy(head, mate, ys - 1).start()
-
-    for dz in z_near + z_later:
-        wait_block(at(2, dz))
-
-    def product(block):
-        width = mixed_in.shape[2]
-        return jnp.dot(
-            mixed_in[block], weight[pl.ds(pl.multiple_of(block * width, width), width), :],
-            preferred_element_type=jnp.float32,
-        )
-
-    total = product(head)
-    for t in range(1, ys):
-        block_copy(along(t), mate, 0).wait_recv()
-        block_copy(along(t), mate, ys - 1 + t).start()
-        total = total + product(along(t))
-    for t in range(ys):
-        block = lax.rem(mate + 2 * t, n_head)
-        block_copy(block, mate, 0).wait_recv()
-        total = total + product(block)
-    out_ref[...] = total.astype(out_ref.dtype)
-
-    @pl.loop(1, n)
-    def _(i):
-        for kind in (LAB, Q, K, V, O):
+        for kind in (LAB, Q, K, V, O, O + 1):
             copy(kind, i).wait_send()
 
     for j in range(parts):
@@ -409,18 +435,18 @@
         def _():
             piece_copy(j).wait_send()
 
-    for i in range(3):
-        z_first_copy(i).wait_send()
-    for i in range(4):
-        z_second_copy(i).wait_send()
+    for way in (1, -1):
+        for distance in range(1, far + 1):
+            z_copy(distance, way).wait_send()
     for dz in range(z_size):
         for i in range(2):
             x_first_copy(dz, i).wait_send()
         x_second_copy(dz).wait_send()
-    for t in range(1, ys):
-        block_copy(head, along(t), t - 1).wait_send()
-        block_copy(along(t), mate, ys - 1 + t).wait_send()
-    block_copy(head, mate, ys - 1).wait_send()
+    for part in range(2):
+        for t in range(1, ys):
+            block_copy(part, head, along(t), t - 1).wait_send()
+            block_copy(part, along(t), mate, ys - 1 + t).wait_send()
+        block_copy(part, head, mate, ys - 1).wait_send()
 
 
 def mix(queries, keys, values, out_weight, query_cluster, key_cluster, cluster_owner, bias):
@@ -445,17 +471,18 @@
             rows(slots_q), rows(slots_q),
             pltpu.VMEM((n, 8, 128), jnp.float32), pltpu.VMEM((n, 8, 128), jnp.float32),
             rows(slots_k), rows(slots_k), rows(slots_k), rows(slots_k),
-            rows(slots_q), rows(slots_q),
+            pltpu.VMEM((2 * slots_q, width // 2), jnp.bfloat16),
+            pltpu.VMEM((2 * slots_q, width // 2), jnp.bfloat16),
             pltpu.VMEM((1, q_rows), jnp.int32), pltpu.VMEM((1, k_rows), jnp.int32),
             pltpu.VMEM((clusters, slots_k), jnp.bfloat16),
             pltpu.VMEM((heads, slots_q, slots_k), jnp.bfloat16),
             pltpu.VMEM((parts, depth, narrow), jnp.bfloat16),
             pltpu.VMEM((depth * n, narrow * parts), jnp.bfloat16),
-            pltpu.VMEM((n_head, q_rows, width), jnp.bfloat16),
-            pltpu.SemaphoreType.DMA((5, n)), pltpu.SemaphoreType.DMA((5, n)),
+            pltpu.VMEM((n_head, 2, q_rows, width // 2), jnp.bfloat16),
+            pltpu.SemaphoreType.DMA((6, n)), pltpu.SemaphoreType.DMA((6, n)),
             pltpu.SemaphoreType.DMA((parts,)), pltpu.SemaphoreType.DMA((parts,)),
-            pltpu.SemaphoreType.DMA((n + 7,)), pltpu.SemaphoreType.DMA((n,)),
-            pltpu.SemaphoreType.DMA((n_head,)), pltpu.SemaphoreType.DMA((n_head,)),
+            pltpu.SemaphoreType.DMA((n,)), pltpu.SemaphoreType.DMA((n + 1,)),
+            pltpu.SemaphoreType.DMA((2, n_head)), pltpu.SemaphoreType.DMA((2, n_head)),
         ],
         compiler_params=pltpu.CompilerParams(
             collective_id=0, has_side_effects=True, vmem_limit_bytes=60 * 2**20

time: 294 us -> 277 us (0.942)
  Pallas kernels: 288 us -> 269 us
    pallas_call x1, Pallas kernels: 288 us -> 269 us  [mix(): pl.pallas_call(functools.partial(exchange_kernel, n, n_head), out_shape=j...]
where the time goes in v3:
time: 277 us; the launch traced here: 275 us
  Pallas kernels  269 us (97%)
  local copies, waits for them, and re-layouts  3.65 us (1%)
    pallas_call x1, Pallas kernels, mix(): pl.pallas_call(functools.partial(exchange_kernel, n, n_head), out_shape=j...  269 us

profile of v3, /device:TPU:1, one launch (start us, length us, event | category | flops | bytes accessed | tf_op | source)
XLA Modules:
  0.0 274.6 jit_solution(1783243042515581478)
XLA Ops:
  0.0 1.0 fusion
  1.0 0.7 select_convert_fusion.bias_ref
  1.7 1.9 copy.11.w_ref
  3.6 269.2 %shard_map.82 = bf16[256,768]{1,0:T(8,128)(2,1)} custom-call(bf16[256,768]{1,0:T(8,128)(2,1)} %q_ref.1, bf16[1024,768]{1,0:T(8,128)(2,1)} %k_ref.1, bf16[1024,768]{1,0:T(8,128)(2,1)} %v_ref.1, bf16[768,192]{1,0:T(8,128)(2,1)} %copy.11.w_ref, s32[1,256]{1,0:T(1,128)} %bitcast.4, s32[1,1024]{1,0:T(1,128)} %bitcast.3, s32[1,128]{1,0:T(1,128)} %bitcast.5, ...), custom_call_target="tpu_custom_call" | custom-call | flops 199999995904 | bytes 16777216 | tf_op jit(solution)/shard_map/pallas_call | solution.py:465
  272.8 1.8 copy.13

commit v4 on v3

--- a/solution.py
+++ b/solution.py
@@ -178,6 +178,8 @@
         for dz in blocks:
             for i in range(2):
                 x_first_copy(dz, i).start()
+
+    z_order = (0, 1, -1, 2, -2, 3, -3, far)
 
     def x_step(dz):
         wait_block(at(1, dz))
@@ -361,9 +363,6 @@
             total = jnp.exp2(-largest * exponent) + jnp.sum(weights, axis=1, keepdims=True)
             probs[h, rows, :] = (weights * (1.0 / total)).astype(jnp.bfloat16)
 
-    for dz in (0, 1, -1, 2, -2):
-        x_step(dz)
-
     @pl.loop(1, n)
     def _(i):
         copy(V, i).wait_recv()
@@ -384,7 +383,7 @@
         own = slice(part * slots_q, part * slots_q + q_cap)
         ro[own, :] = so[own, :]
 
-    for dz in (3, -3, far):
+    for dz in z_order:
         x_step(dz)
 
     unpack = hot(iota((slots_q, q_rows), 0) == q_slot[...])

time: 277 us -> 269 us (0.971)
  Pallas kernels: 269 us -> 261 us
    pallas_call x1, Pallas kernels: 269 us -> 261 us  [mix(): pl.pallas_call(functools.partial(exchange_kernel, n, n_head), out_shape=j...]
where the time goes in v4:
time: 269 us; the launch traced here: 266 us
  Pallas kernels  261 us (97%)
  local copies, waits for them, and re-layouts  3.65 us (1%)
    pallas_call x1, Pallas kernels, mix(): pl.pallas_call(functools.partial(exchange_kernel, n, n_head), out_shape=j...  261 us

profile of v4, /device:TPU:1, one launch (start us, length us, event | category | flops | bytes accessed | tf_op | source)
XLA Modules:
  0.0 266.3 jit_solution(8376713116510547364)
XLA Ops:
  0.0 1.0 fusion
  1.0 0.7 select_convert_fusion.bias_ref
  1.7 1.9 copy.11.w_ref
  3.6 260.9 %shard_map.82 = bf16[256,768]{1,0:T(8,128)(2,1)} custom-call(bf16[256,768]{1,0:T(8,128)(2,1)} %q_ref.1, bf16[1024,768]{1,0:T(8,128)(2,1)} %k_ref.1, bf16[1024,768]{1,0:T(8,128)(2,1)} %v_ref.1, bf16[768,192]{1,0:T(8,128)(2,1)} %copy.11.w_ref, s32[1,256]{1,0:T(1,128)} %bitcast.4, s32[1,1024]{1,0:T(1,128)} %bitcast.3, s32[1,128]{1,0:T(1,128)} %bitcast.5, ...), custom_call_target="tpu_custom_call" | custom-call | flops 199999995904 | bytes 16777216 | tf_op jit(solution)/shard_map/pallas_call | solution.py:464
  264.5 1.8 copy.13
